TPU v7x, 256 devices: a whole 4x4x8 slice. The times are simulated.
256 devices in a mesh: gx: 4 (over y), gy: 16 (over z, core), gz: 4 (over x).
Axes of the slice: x: 4, y: 4, z: 8, core: 2. Of those that a mesh axis runs over, the one named last changes fastest.
Arguments:
- orbitals: float32 [4, 128, 256, 512], P(None, 'gz', 'gy', 'gx'), may hold values from -20 to 20
- potential: float32 [128, 256, 512], P('gz', 'gy', 'gx'), may hold values from -1.5 to 1.5
Outputs:
- orthonormal: float32 [4, 128, 256, 512], P(None, 'gz', 'gy', 'gx')
- factor: float32 [4, 4], replicated
All inputs are finite; a program needn't handle non-finite values.
Results may differ from a plain program's by a relative error of at most 0.0003.
Values sent between devices are 32-bit elements; how exact they have to be, the bound alone decides.
A program may use at most 128 MiB of HBM per device.

v0:
```python
import functools

import jax
import jax.numpy as jnp
from jax import lax
from jax.experimental import pallas as pl
from jax.experimental.pallas import tpu as pltpu
from jax.sharding import PartitionSpec as P

DEG = 3
REACH = 4
LANES = 128
ROWS = 8
MESH = pl.DeviceIdType.MESH

stencil_weights = (-205.0 / 72.0, 8.0 / 5.0, -1.0 / 5.0, 8.0 / 315.0, -1.0 / 560.0)
lower_end = -1.5
cutoff = 3.0
upper_end = 12.0
half_width = (upper_end - cutoff) / 2.0
centre = (upper_end + cutoff) / 2.0
sigma_first = half_width / (lower_end - centre)


def recurrence():
    steps = [(sigma_first / half_width, 0.0)]
    sigma = sigma_first
    for _ in range(DEG - 1):
        sigma_new = 1.0 / (2.0 / sigma_first - sigma)
        steps.append((2.0 * sigma_new / half_width, sigma * sigma_new))
        sigma = sigma_new
    return steps


def edge_matrices():
    scaled = [round(5040.0 * weight) for weight in stencil_weights]
    row = lax.broadcasted_iota(jnp.int32, (2 * LANES, LANES), 0)
    col = lax.broadcasted_iota(jnp.int32, (2 * LANES, LANES), 1)
    part = row % ROWS
    edge = jnp.where(part < REACH, part - REACH, LANES - REACH + part)
    apart = jnp.abs(jnp.where(row < LANES, row, edge) - col)
    matrix = jnp.zeros((2 * LANES, LANES), jnp.float32)
    for k in range(1, REACH + 1):
        matrix = jnp.where(apart == k, float(scaled[k]), matrix)
    return matrix.astype(jnp.bfloat16)


def place_mask(vectors):
    row = lax.broadcasted_iota(jnp.int32, (vectors * ROWS, LANES), 0)
    col = lax.broadcasted_iota(jnp.int32, (vectors * ROWS, LANES), 1)
    return jnp.where(row // ROWS == col // ROWS, 1.0, 0.0).astype(jnp.bfloat16)


def thirds(value):
    first = value.astype(jnp.bfloat16)
    rest = value - first.astype(jnp.float32)
    second = rest.astype(jnp.bfloat16)
    third = (rest - second.astype(jnp.float32)).astype(jnp.bfloat16)
    return first, second, third


def filter_kernel(
    sizes,
    orbitals,
    potential,
    filtered,
    gram,
    field,
    raw,
    base,
    diagonal,
    x_send,
    x_recv,
    matrix,
    mask,
    partial,
    sums,
    load_sem,
    send_sem,
    recv_sem,
    gram_send_sem,
    gram_recv_sem,
    near_sem,
    line_sem,
    plane_sem,
):
    count_x, count_y, count_z = sizes
    norb, size_z, size_y = orbitals.shape[:3]
    groups = size_z // ROWS
    tiles = size_y // ROWS
    me_x, me_y, me_z = (lax.axis_index(a) for a in ("gx", "gy", "gz"))

    def at(dx, dy, dz):
        return (
            lax.rem(me_x + dx, count_x),
            lax.rem(me_y + dy, count_y),
            lax.rem(me_z + dz, count_z),
        )

    def greet(sem, offsets):
        for there in offsets:
            pl.semaphore_signal(sem, inc=1, device_id=at(*there), device_id_type=MESH)

    beside = [
        (1, 0, 0),
        (count_x - 1, 0, 0),
        (0, 1, 0),
        (0, count_y - 1, 0),
        (0, 0, 1),
        (0, 0, count_z - 1),
    ]
    near = [(2, 0, 0), (0, 2, 0), (0, count_y - 2, 0), (0, 0, 2)]
    line = [(0, 4, 0), (0, count_y - 4, 0)]
    plane = [(dx, 0, dz) for dx in range(count_x) for dz in range(count_z)][1:]

    barrier = pltpu.get_barrier_semaphore()
    greet(barrier, beside)

    body_z = pl.ds(REACH, size_z)
    body_y = pl.ds(ROWS, size_y)

    loads = [
        pltpu.make_async_copy(
            orbitals.at[o], field.at[0, o, body_z, body_y], load_sem.at[o]
        )
        for o in range(norb)
    ]
    loads.append(pltpu.make_async_copy(potential, raw, load_sem.at[norb]))
    for load in loads:
        load.start()

    lane = lax.broadcasted_iota(jnp.int32, (ROWS, LANES), 1)
    matrix[...] = edge_matrices()
    mask[...] = place_mask(ROWS * tiles)
    partial[...] = jnp.zeros_like(partial)

    def face_copies(step, o):
        def remote(src, dst, kind, there):
            return pltpu.make_async_remote_copy(
                src_ref=src,
                dst_ref=dst,
                send_sem=send_sem.at[step, o, kind],
                recv_sem=recv_sem.at[step, o, kind],
                device_id=at(*there),
                device_id_type=MESH,
            )

        def layers(first):
            return field.at[step, o, pl.ds(first, REACH), body_y]

        def rows(first):
            return field.at[step, o, body_z, pl.ds(first, REACH)]

        return [
            remote(rows(ROWS), rows(ROWS + size_y), 0, (0, count_y - 1, 0)),
            remote(rows(ROWS + size_y - REACH), rows(ROWS - REACH), 0, (0, 1, 0)),
            remote(layers(REACH), layers(REACH + size_z), 1, (0, 0, count_z - 1)),
            remote(layers(size_z), layers(0), 1, (0, 0, 1)),
            remote(x_send.at[step, o], x_recv.at[step, o, 1], 2, (count_x - 1, 0, 0)),
            remote(x_send.at[step, o], x_recv.at[step, o, 0], 2, (1, 0, 0)),
        ]

    def send_faces(step, o):
        for copy in face_copies(step, o):
            copy.start()

    def wait_faces(sem, step, o):
        for kind, span in (
            (0, field.at[step, o, body_z, pl.ds(0, 2 * REACH)]),
            (1, field.at[step, o, pl.ds(0, 2 * REACH), body_y]),
            (2, x_recv.at[step, o]),
        ):
            pltpu.make_async_copy(span, span, sem.at[step, o, kind]).wait()

    def put_edges(place, value, packed):
        moved = pltpu.roll(value, (REACH + ROWS * place) % LANES, 1)
        return jnp.where(lane // ROWS == place, moved, packed)

    def pack(o):
        def group(g, _):
            packed = jnp.zeros((ROWS, LANES), jnp.float32)
            for zz in range(ROWS):
                for tile in range(tiles):
                    z = g * ROWS + zz
                    value = field[0, o, REACH + z, pl.ds(ROWS * (1 + tile), ROWS)]
                    packed = put_edges(zz * tiles + tile, value, packed)
            x_send[0, o, g] = packed
            return 0

        lax.fori_loop(0, groups, group, 0, unroll=2)

    for o in range(norb):
        loads[o].wait()
        pack(o)
        if o == 0:
            pl.semaphore_wait(barrier, len(beside))
        send_faces(0, o)

    loads[norb].wait()
    steps = recurrence()

    def settle(z, _):
        level = raw[z] + (-1.5 * stencil_weights[0] - centre)
        for step, (alpha, _) in enumerate(steps):
            diagonal[step, z] = alpha * level
        return 0

    lax.fori_loop(0, size_z, settle, 0, unroll=4)

    def weights_of(alpha):
        return [alpha * (-0.5 * weight) for weight in stencil_weights], alpha * (-0.5 / 5040.0)

    def prepare(step, o, alpha, gamma):
        weights, from_scaled = weights_of(alpha)
        for g in range(groups):
            inside = field[step, o, pl.ds(REACH + ROWS * g, ROWS), body_y].reshape(-1, LANES)
            along_x = None
            for cells in thirds(inside):
                term = jnp.dot(cells, matrix[:LANES], preferred_element_type=jnp.float32)
                along_x = term if along_x is None else along_x + term
            along_x = along_x.reshape(ROWS, tiles, ROWS, LANES)
            for tile in range(tiles):
                first = ROWS * (1 + tile)
                inward = 1 - 2 * tile
                planes = {
                    z: field[step, o, REACH + z, pl.ds(first, ROWS)]
                    for z in range(ROWS * g - REACH, ROWS * (g + 1) + REACH)
                    if 0 <= z < size_z
                }
                for zz in range(ROWS):
                    z = ROWS * g + zz
                    total = diagonal[step, z, pl.ds(ROWS * tile, ROWS)] * planes[z]
                    total += from_scaled * along_x[zz, tile]
                    for k in range(1, REACH + 1):
                        around = field[step, o, REACH + z, pl.ds(first + inward * k, ROWS)]
                        for other in (z - k, z + k):
                            if other in planes:
                                around += planes[other]
                        total += weights[k] * around
                    if gamma is not None:
                        total -= gamma * field[step - 1, o, REACH + z, pl.ds(first, ROWS)]
                    base[o, z, pl.ds(ROWS * tile, ROWS)] = total

    def finish(step, o, alpha, last):
        weights, from_scaled = weights_of(alpha)
        for g in range(groups):
            edges = jnp.where(
                lane % ROWS < REACH, x_recv[step, o, 0, g], x_recv[step, o, 1, g]
            )
            ends = [
                jnp.concatenate([part] * (ROWS * tiles), 0) * mask[...] for part in thirds(edges)
            ]
            outside = matrix[LANES:]
            along_x = jnp.dot(
                jnp.concatenate(ends[:2], 1),
                jnp.concatenate([outside, outside], 0),
                preferred_element_type=jnp.float32,
            ) + jnp.dot(ends[2], outside, preferred_element_type=jnp.float32)
            along_x = along_x.reshape(ROWS, tiles, ROWS, LANES)
            packed = jnp.zeros((ROWS, LANES), jnp.float32)
            for tile in range(tiles):
                first = ROWS * (1 + tile)
                outward = 2 * tile - 1
                for zz in range(ROWS):
                    z = ROWS * g + zz
                    total = base[o, z, pl.ds(ROWS * tile, ROWS)] + from_scaled * along_x[zz, tile]
                    for k in range(1, REACH + 1):
                        around = field[step, o, REACH + z, pl.ds(first + outward * k, ROWS)]
                        for other in (z - k, z + k):
                            if not 0 <= other < size_z:
                                around += field[step, o, REACH + other, pl.ds(first, ROWS)]
                        total += weights[k] * around
                    if last:
                        filtered[o, z, pl.ds(ROWS * tile, ROWS)] = total
                    else:
                        field[step + 1, o, REACH + z, pl.ds(first, ROWS)] = total
                        packed = put_edges(zz * tiles + tile, total, packed)
            if not last:
                x_send[step + 1, o, g] = packed

    def begin(o, _):
        prepare(0, o, steps[0][0], None)
        return 0

    lax.fori_loop(0, norb, begin, 0)

    def early(q, _):
        step, o = q // norb, lax.rem(q, norb)
        wait_faces(recv_sem, step, o)

        @pl.when(q == 0)
        def _():
            greet(near_sem, near)

        finish(step, o, jnp.where(step == 0, steps[0][0], steps[1][0]), False)
        send_faces(step + 1, o)
        alpha, gamma = (
            jnp.where(step == 0, first, second) for first, second in zip(steps[1], steps[2])
        )
        prepare(step + 1, o, alpha, gamma)

        @pl.when(q == norb - 1)
        def _():
            pl.semaphore_wait(near_sem, len(near))
            greet(line_sem, line)

        @pl.when(q == (DEG - 1) * norb - 1)
        def _():
            pl.semaphore_wait(line_sem, len(line))
            greet(plane_sem, plane)

        return 0

    lax.fori_loop(0, (DEG - 1) * norb, early, 0)

    def gram_row(o):
        def add(z, totals):
            for tile in range(tiles):
                rows = pl.ds(ROWS * tile, ROWS)
                mine = filtered[o, z, rows]
                totals = tuple(
                    totals[b] + mine * (mine if b == o else filtered[b, z, rows])
                    for b in range(o + 1)
                )
            return totals

        start = (jnp.zeros((ROWS, LANES), jnp.float32),) * (o + 1)
        totals = lax.fori_loop(0, size_z, add, start, unroll=8)
        for b in range(o + 1):
            partial[o * norb + b] = totals[b]

    def late(o, _):
        wait_faces(recv_sem, DEG - 1, o)
        finish(DEG - 1, o, steps[DEG - 1][0], True)
        for k in range(norb):
            pl.when(o == k)(functools.partial(gram_row, k))
        return 0

    lax.fori_loop(0, norb, late, 0)

    own = jnp.zeros((ROWS, LANES), jnp.float32)
    for a in range(norb):
        for b in range(a + 1):
            pair = a * norb + b
            own = jnp.where(lane == pair, jnp.sum(partial[pair], axis=1, keepdims=True), own)
    slot = (me_x * count_y + me_y) * count_z + me_z
    sums[slot] = jnp.sum(own, axis=0, keepdims=True)

    pl.semaphore_wait(plane_sem, len(plane))

    def share(dy, there):
        pltpu.make_async_remote_copy(
            src_ref=sums.at[slot],
            dst_ref=sums.at[slot],
            send_sem=gram_send_sem,
            recv_sem=gram_recv_sem,
            device_id=at(there[0], dy, there[1]),
            device_id_type=MESH,
        ).start()

    by_plane = sorted(
        ((dx, dz) for dx in range(count_x) for dz in range(count_z)),
        key=lambda d: -min(d[0], count_x - d[0]) - min(d[1], count_z - d[1]),
    )

    def far_line(i, _):
        dy = count_y // 2 + (1 - 2 * lax.rem(i, 2)) * ((i + 1) // 2)
        for there in by_plane:
            share(dy, there)
        return 0

    lax.fori_loop(0, count_y - 1, far_line, 0)
    for there in by_plane[:-1]:
        share(0, there)

    def drain(i, _):
        wait_faces(send_sem, i // norb, lax.rem(i, norb))
        return 0

    lax.fori_loop(0, DEG * norb, drain, 0)

    devices = count_x * count_y * count_z
    others = sums.at[pl.ds(0, devices - 1)]
    pltpu.make_async_copy(others, others, gram_recv_sem).wait()

    width = 16

    def add_up(i, total):
        return total + sums[pl.ds(pl.multiple_of(i * width, width), width)]

    total = lax.fori_loop(1, devices // width, add_up, sums[pl.ds(0, width)], unroll=5)
    while total.shape[0] > 1:
        half = total.shape[0] // 2
        total = total[:half] + total[half:]
    gram[...] = total[0]
    pltpu.make_async_copy(others, others, gram_send_sem).wait()


def combine_kernel(ncells, gram, filtered, result, factor, out, store_sem):
    norb, size_z, size_y = filtered.shape[:3]
    lane = lax.broadcasted_iota(jnp.int32, (ROWS, LANES), 1)
    sums = jnp.broadcast_to(gram[...], (ROWS, LANES))

    def entry(a, b):
        pair = max(a, b) * norb + min(a, b)
        value = jnp.sum(jnp.where(lane == pair, sums, 0.0), axis=1, keepdims=True)
        return jnp.broadcast_to(value, (ROWS, LANES)) / ncells

    upper = [[None] * norb for _ in range(norb)]
    inverse = [[None] * norb for _ in range(norb)]
    for i in range(norb):
        for j in range(i, norb):
            rest = entry(i, j)
            for m in range(i):
                rest = rest - upper[m][i] * upper[m][j]
            if i == j:
                upper[i][i] = jnp.sqrt(rest)
                inverse[i][i] = 1.0 / upper[i][i]
            else:
                upper[i][j] = rest * inverse[i][i]
    for i in reversed(range(norb)):
        for j in range(i + 1, norb):
            rest = upper[i][i + 1] * inverse[i + 1][j]
            for m in range(i + 2, j + 1):
                rest = rest + upper[i][m] * inverse[m][j]
            inverse[i][j] = -rest * inverse[i][i]

    row = lax.broadcasted_iota(jnp.int32, (norb, norb), 0)
    col = lax.broadcasted_iota(jnp.int32, (norb, norb), 1)
    matrix = jnp.zeros((norb, norb), jnp.float32)
    for i in range(norb):
        for j in range(i, norb):
            matrix = jnp.where((row == i) & (col == j), upper[i][j][:norb, :norb], matrix)
    factor[...] = matrix

    chunks = store_sem.shape[0]
    length = size_z // chunks
    stores = []
    for c in range(chunks):

        def one(z, _):
            for tile in range(size_y // ROWS):
                rows = pl.ds(ROWS * tile, ROWS)
                held = [filtered[a, z, rows] for a in range(norb)]
                for b in range(norb):
                    total = held[0] * inverse[0][b]
                    for a in range(1, b + 1):
                        total = total + held[a] * inverse[a][b]
                    out[b, z, rows] = total
            return 0

        lax.fori_loop(c * length, (c + 1) * length, one, 0, unroll=4)
        part = pl.ds(c * length, length)
        stores.append(
            pltpu.make_async_copy(out.at[:, part], result.at[:, part], store_sem.at[c])
        )
        stores[-1].start()
    for store in stores:
        store.wait()


def per_device(sizes, ncells, orbitals, potential):
    norb, size_z, size_y, size_x = orbitals.shape
    assert size_x == LANES and size_z % ROWS == 0 and size_y == 2 * ROWS
    assert sizes == (4, 16, 4)
    hbm = pl.BlockSpec(memory_space=pltpu.HBM)
    vmem = pl.BlockSpec(memory_space=pltpu.VMEM)
    f32 = jnp.float32
    groups = size_z // ROWS
    devices = sizes[0] * sizes[1] * sizes[2]
    orbitals = pltpu.with_memory_space_constraint(orbitals, pltpu.HBM)
    potential = pltpu.with_memory_space_constraint(potential, pltpu.HBM)
    filtered, gram = pl.pallas_call(
        functools.partial(filter_kernel, sizes),
        out_shape=(
            jax.ShapeDtypeStruct(orbitals.shape, f32),
            jax.ShapeDtypeStruct((1, LANES), f32),
        ),
        in_specs=[hbm, hbm],
        out_specs=(vmem, vmem),
        scratch_shapes=[
            pltpu.VMEM((DEG, norb, size_z + 2 * REACH, size_y + 2 * ROWS, LANES), f32),
            pltpu.VMEM((size_z, size_y, LANES), f32),
            pltpu.VMEM(orbitals.shape, f32),
            pltpu.VMEM((DEG, size_z, size_y, LANES), f32),
            pltpu.VMEM((DEG, norb, groups, ROWS, LANES), f32),
            pltpu.VMEM((DEG, norb, 2, groups, ROWS, LANES), f32),
            pltpu.VMEM((2 * LANES, LANES), jnp.bfloat16),
            pltpu.VMEM((ROWS * size_y, LANES), jnp.bfloat16),
            pltpu.VMEM((norb * norb, ROWS, LANES), f32),
            pltpu.VMEM((devices, 1, LANES), f32),
            pltpu.SemaphoreType.DMA((norb + 1,)),
            pltpu.SemaphoreType.DMA((DEG, norb, 3)),
            pltpu.SemaphoreType.DMA((DEG, norb, 3)),
            pltpu.SemaphoreType.DMA,
            pltpu.SemaphoreType.DMA,
            pltpu.SemaphoreType.REGULAR,
            pltpu.SemaphoreType.REGULAR,
            pltpu.SemaphoreType.REGULAR,
        ],
        compiler_params=pltpu.CompilerParams(
            collective_id=0, has_side_effects=True, vmem_limit_bytes=32 * 2**20
        ),
        name="filter_and_gram",
    )(orbitals, potential)
    return pl.pallas_call(
        functools.partial(combine_kernel, ncells),
        out_shape=(
            jax.ShapeDtypeStruct(orbitals.shape, f32),
            jax.ShapeDtypeStruct((norb, norb), f32),
        ),
        in_specs=[vmem, vmem],
        out_specs=(hbm, vmem),
        scratch_shapes=[
            pltpu.VMEM(orbitals.shape, f32),
            pltpu.SemaphoreType.DMA((4,)),
        ],
        compiler_params=pltpu.CompilerParams(vmem_limit_bytes=16 * 2**20),
        name="combine",
    )(gram, filtered)


def solution(mesh):
    sizes = tuple(mesh.shape[a] for a in ("gx", "gy", "gz"))

    def run(orbitals, potential):
        ncells = float(potential.size)
        return jax.shard_map(
            functools.partial(per_device, sizes, ncells),
            mesh=mesh,
            in_specs=(P(None, "gz", "gy", "gx"), P("gz", "gy", "gx")),
            out_specs=(P(None, "gz", "gy", "gx"), P()),
            check_vma=False,
        )(orbitals, potential)

    return run
```

profile of v0, /device:TPU:1, one launch (start us, length us, event | category | flops | bytes accessed | tf_op | source)
XLA Modules:
  0.0 34.9 jit_solution(9893842029874184017)
XLA Ops:
  0.6 32.5 %filter_and_gram.1 = (f32[4,32,16,128]{3,2,1,0:T(8,128)S(1)}, f32[1,128]{1,0:T(1,128)S(1)}) custom-call(f32[4,32,16,128]{3,2,1,0:T(8,128)} %orbitals.1, f32[32,16,128]{2,1,0:T(8,128)} %potential.1), custom_call_target="tpu_custom_call" | custom-call | tf_op jit(solution)/shard_map/filter_and_gram/pallas_call | solution.py:473
  33.1 1.8 %combine.1 = (f32[4,32,16,128]{3,2,1,0:T(8,128)}, f32[4,4]{1,0:T(4,128)}) custom-call(f32[1,128]{1,0:T(1,128)S(1)} %get-tuple-element.4.gram, f32[4,32,16,128]{3,2,1,0:T(8,128)S(1)} %get-tuple-element.5.filtered), custom_call_target="tpu_custom_call" | custom-call | tf_op jit(solution)/shard_map/combine/pallas_call | solution.py:506
where the time goes:
time: 35 us; the launch traced here: 34.9 us
  Pallas kernels  34.2 us (98%)
  between operations  0.64 us (2%)
    pallas_call x1, Pallas kernels, per_device(): pl.pallas_call(functools.partial(filter_kernel, sizes), out_shape=(jax.Sh...  32.5 us
    pallas_call x1, Pallas kernels, per_device(): pl.pallas_call(functools.partial(combine_kernel, ncells), out_shape=(jax....  1.77 us

commit v1 on v0

--- a/solution.py
+++ b/solution.py
@@ -152,12 +152,12 @@
             return field.at[step, o, body_z, pl.ds(first, REACH)]
 
         return [
+            remote(x_send.at[step, o], x_recv.at[step, o, 1], 2, (count_x - 1, 0, 0)),
+            remote(x_send.at[step, o], x_recv.at[step, o, 0], 2, (1, 0, 0)),
+            remote(layers(REACH), layers(REACH + size_z), 1, (0, 0, count_z - 1)),
+            remote(layers(size_z), layers(0), 1, (0, 0, 1)),
             remote(rows(ROWS), rows(ROWS + size_y), 0, (0, count_y - 1, 0)),
             remote(rows(ROWS + size_y - REACH), rows(ROWS - REACH), 0, (0, 1, 0)),
-            remote(layers(REACH), layers(REACH + size_z), 1, (0, 0, count_z - 1)),
-            remote(layers(size_z), layers(0), 1, (0, 0, 1)),
-            remote(x_send.at[step, o], x_recv.at[step, o, 1], 2, (count_x - 1, 0, 0)),
-            remote(x_send.at[step, o], x_recv.at[step, o, 0], 2, (1, 0, 0)),
         ]
 
     def send_faces(step, o):
@@ -315,19 +315,19 @@
 
     def gram_row(o):
         def add(z, totals):
+            fresh = []
             for tile in range(tiles):
                 rows = pl.ds(ROWS * tile, ROWS)
                 mine = filtered[o, z, rows]
-                totals = tuple(
-                    totals[b] + mine * (mine if b == o else filtered[b, z, rows])
-                    for b in range(o + 1)
-                )
-            return totals
-
-        start = (jnp.zeros((ROWS, LANES), jnp.float32),) * (o + 1)
-        totals = lax.fori_loop(0, size_z, add, start, unroll=8)
+                for b in range(o + 1):
+                    other = mine if b == o else filtered[b, z, rows]
+                    fresh.append(totals[len(fresh)] + mine * other)
+            return tuple(fresh)
+
+        start = (jnp.zeros((ROWS, LANES), jnp.float32),) * (tiles * (o + 1))
+        totals = lax.fori_loop(0, size_z, add, start, unroll=16)
         for b in range(o + 1):
-            partial[o * norb + b] = totals[b]
+            partial[o * norb + b] = sum(totals[b + o + 1 :: o + 1], totals[b])
 
     def late(o, _):
         wait_faces(recv_sem, DEG - 1, o)
@@ -344,34 +344,38 @@
             pair = a * norb + b
             own = jnp.where(lane == pair, jnp.sum(partial[pair], axis=1, keepdims=True), own)
     slot = (me_x * count_y + me_y) * count_z + me_z
-    sums[slot] = jnp.sum(own, axis=0, keepdims=True)
+    sums[pl.ds(slot, 1)] = jnp.sum(own, axis=0, keepdims=True)
 
     pl.semaphore_wait(plane_sem, len(plane))
 
-    def share(dy, there):
+    chips = count_y // 2
+    chip, core = me_y // 2, lax.rem(me_y, 2)
+    xs = [lax.rem(me_x + d, count_x) for d in range(count_x)]
+    zs = [lax.rem(me_z + d, count_z) for d in range(count_z)]
+    ys = []
+    for d in range(chips):
+        start = 2 * lax.rem(chip + d, chips)
+        ys.append((start + core, start + 1 - core))
+
+    def hops(there):
+        return sum(min(d, n - d) for d, n in zip(there[:3], (count_x, chips, count_z)))
+
+    everyone = [
+        (dx, dc, dz, other)
+        for dx in range(count_x)
+        for dc in range(chips)
+        for dz in range(count_z)
+        for other in range(2)
+    ]
+    for dx, dc, dz, other in sorted(everyone[1:], key=hops, reverse=True):
         pltpu.make_async_remote_copy(
-            src_ref=sums.at[slot],
-            dst_ref=sums.at[slot],
+            src_ref=sums.at[pl.ds(slot, 1)],
+            dst_ref=sums.at[pl.ds(slot, 1)],
             send_sem=gram_send_sem,
             recv_sem=gram_recv_sem,
-            device_id=at(there[0], dy, there[1]),
+            device_id=(xs[dx], ys[dc][other], zs[dz]),
             device_id_type=MESH,
         ).start()
-
-    by_plane = sorted(
-        ((dx, dz) for dx in range(count_x) for dz in range(count_z)),
-        key=lambda d: -min(d[0], count_x - d[0]) - min(d[1], count_z - d[1]),
-    )
-
-    def far_line(i, _):
-        dy = count_y // 2 + (1 - 2 * lax.rem(i, 2)) * ((i + 1) // 2)
-        for there in by_plane:
-            share(dy, there)
-        return 0
-
-    lax.fori_loop(0, count_y - 1, far_line, 0)
-    for there in by_plane[:-1]:
-        share(0, there)
 
     def drain(i, _):
         wait_faces(send_sem, i // norb, lax.rem(i, norb))
@@ -383,20 +387,14 @@
     others = sums.at[pl.ds(0, devices - 1)]
     pltpu.make_async_copy(others, others, gram_recv_sem).wait()
 
-    width = 16
-
-    def add_up(i, total):
-        return total + sums[pl.ds(pl.multiple_of(i * width, width), width)]
-
-    total = lax.fori_loop(1, devices // width, add_up, sums[pl.ds(0, width)], unroll=5)
-    while total.shape[0] > 1:
-        half = total.shape[0] // 2
-        total = total[:half] + total[half:]
-    gram[...] = total[0]
+    total = [sums[pl.ds(ROWS * i, ROWS)] for i in range(devices // ROWS)]
+    while len(total) > 1:
+        total = [one + two for one, two in zip(total[::2], total[1::2])]
+    gram[...] = jnp.sum(total[0], axis=0, keepdims=True)
     pltpu.make_async_copy(others, others, gram_send_sem).wait()
 
 
-def combine_kernel(ncells, gram, filtered, result, factor, out, store_sem):
+def combine_kernel(ncells, gram, filtered, result, factor, out, upper_held, store_sem, factor_sem):
     norb, size_z, size_y = filtered.shape[:3]
     lane = lax.broadcasted_iota(jnp.int32, (ROWS, LANES), 1)
     sums = jnp.broadcast_to(gram[...], (ROWS, LANES))
@@ -431,7 +429,9 @@
     for i in range(norb):
         for j in range(i, norb):
             matrix = jnp.where((row == i) & (col == j), upper[i][j][:norb, :norb], matrix)
-    factor[...] = matrix
+    upper_held[...] = matrix
+    factor_store = pltpu.make_async_copy(upper_held, factor, factor_sem)
+    factor_store.start()
 
     chunks = store_sem.shape[0]
     length = size_z // chunks
@@ -455,7 +455,7 @@
             pltpu.make_async_copy(out.at[:, part], result.at[:, part], store_sem.at[c])
         )
         stores[-1].start()
-    for store in stores:
+    for store in [*stores, factor_store]:
         store.wait()
 
 
@@ -488,7 +488,7 @@
             pltpu.VMEM((2 * LANES, LANES), jnp.bfloat16),
             pltpu.VMEM((ROWS * size_y, LANES), jnp.bfloat16),
             pltpu.VMEM((norb * norb, ROWS, LANES), f32),
-            pltpu.VMEM((devices, 1, LANES), f32),
+            pltpu.VMEM((devices, LANES), f32),
             pltpu.SemaphoreType.DMA((norb + 1,)),
             pltpu.SemaphoreType.DMA((DEG, norb, 3)),
             pltpu.SemaphoreType.DMA((DEG, norb, 3)),
@@ -510,10 +510,12 @@
             jax.ShapeDtypeStruct((norb, norb), f32),
         ),
         in_specs=[vmem, vmem],
-        out_specs=(hbm, vmem),
+        out_specs=(hbm, hbm),
         scratch_shapes=[
             pltpu.VMEM(orbitals.shape, f32),
+            pltpu.VMEM((norb, norb), f32),
             pltpu.SemaphoreType.DMA((4,)),
+            pltpu.SemaphoreType.DMA,
         ],
         compiler_params=pltpu.CompilerParams(vmem_limit_bytes=16 * 2**20),
         name="combine",

time: 35 us -> 33.9 us (0.969)
  Pallas kernels: 34.2 us -> 33.2 us
    pallas_call x1, Pallas kernels: 1.77 us -> 1.2 us  [per_device(): pl.pallas_call(functools.partial(combine_kernel, ncells), out_shape=(jax....]
    pallas_call x1, Pallas kernels: 32.5 us -> 32 us  [per_device(): pl.pallas_call(functools.partial(filter_kernel, sizes), out_shape=(jax.Sh...]
where the time goes in v1:
time: 33.9 us; the launch traced here: 33.8 us
  Pallas kernels  33.2 us (98%)
  between operations  0.64 us (2%)
    pallas_call x1, Pallas kernels, per_device(): pl.pallas_call(functools.partial(filter_kernel, sizes), out_shape=(jax.Sh...  32 us
    pallas_call x1, Pallas kernels, per_device(): pl.pallas_call(functools.partial(combine_kernel, ncells), out_shape=(jax....  1.2 us

profile of v1, /device:TPU:1, one launch (start us, length us, event | category | flops | bytes accessed | tf_op | source)
XLA Modules:
  0.0 33.8 jit_solution(580537004389646312)
XLA Ops:
  0.6 32.0 %filter_and_gram.1 = (f32[4,32,16,128]{3,2,1,0:T(8,128)S(1)}, f32[1,128]{1,0:T(1,128)S(1)}) custom-call(f32[4,32,16,128]{3,2,1,0:T(8,128)} %orbitals.1, f32[32,16,128]{2,1,0:T(8,128)} %potential.1), custom_call_target="tpu_custom_call" | custom-call | tf_op jit(solution)/shard_map/filter_and_gram/pallas_call | solution.py:473
  32.6 1.2 %combine.1 = (f32[4,32,16,128]{3,2,1,0:T(8,128)}, f32[4,4]{1,0:T(4,128)}) custom-call(f32[1,128]{1,0:T(1,128)S(1)} %get-tuple-element.4.gram, f32[4,32,16,128]{3,2,1,0:T(8,128)S(1)} %get-tuple-element.5.filtered), custom_call_target="tpu_custom_call" | custom-call | tf_op jit(solution)/shard_map/combine/pallas_call | solution.py:506
